TPU v7x, 256 devices: a whole 4x4x8 slice. The times are simulated.
256 devices in a mesh: dp: 32 (over x_hi, z, core), seq: 8 (over y, x_lo).
Axes of the slice: x: 4 (x_hi: 2, x_lo: 2; x = x_hi * 2 + x_lo), y: 4, z: 8, core: 2. Of those that a mesh axis runs over, the one named last changes fastest.
Arguments:
- inputs: bfloat16 [32, 1024, 1536], P('dp', 'seq'), may hold values from -6 to 6
- saved: bfloat16 [32, 1024, 1536], P('dp', 'seq'), may hold values from -32 to 32
- attn_saved: bfloat16 [32, 1024, 1536], P('dp', 'seq'), may hold values from -6 to 6
- upstream: bfloat16 [32, 1024, 1536], P('dp', 'seq'), may hold values from -6 to 6
- w_qkv: bfloat16 [1536, 3, 1536], P(None, None, 'seq'), may hold values from -0.15625 to 0.15625
- w_out: bfloat16 [1536, 1536], P('seq'), may hold values from -0.15625 to 0.15625
- w_conv: bfloat16 [5, 1536, 1536], P(None, ('seq', 'dp')), may hold values from -0.0625 to 0.0625
Outputs:
- grad_inputs: bfloat16 [32, 1024, 1536], P('dp', 'seq')
- grad_qkv: bfloat16 [1536, 3, 1536], P('dp', None, 'seq')
- grad_out: bfloat16 [1536, 1536], P(('seq', 'dp'))
- grad_conv: bfloat16 [5, 1536, 1536], P(None, ('seq', 'dp'))
All inputs are finite; a program needn't handle non-finite values.
Results may differ from a plain program's by a relative error of at most 0.034.
Values may be sent and summed in bfloat16 or wider, within the bound.
A program may use at most 128 MiB of HBM per device.

v0:
```python
import math

import jax
import jax.numpy as jnp
from jax import lax
from jax.experimental import pallas as pl
from jax.experimental.pallas import tpu as pltpu
from jax.sharding import PartitionSpec as P

HD = 192
TAPS = 5
DILATION = 32
EPSILON = 1e-06
REACH = DILATION * (TAPS // 2)
BF16 = jnp.bfloat16
F32 = jnp.float32
MESH = pl.DeviceIdType.MESH
VMEM = pltpu.VMEM
ANY = pl.ANY


def seq_at(dy, dx):
    here = lax.axis_index("seq")
    return lax.rem(here // 2 + dy, 4) * 2 + lax.rem(here + dx, 2)


def dp_at(dxh, dz, dcore):
    here = lax.axis_index("dp")
    core = lax.rem(here + dcore, 2)
    z = lax.rem(here // 2 + dz, 8)
    xh = lax.rem(here // 16 + dxh, 2)
    return (xh * 8 + z) * 2 + core


SEQ_OFFSETS = [(dy, dx) for dy in (2, 1, 3, 0) for dx in (1, 0) if (dy, dx) != (0, 0)]


def meet(peers):
    barrier = pltpu.get_barrier_semaphore()
    for peer in peers:
        pl.semaphore_signal(barrier, inc=1, device_id=peer, device_id_type=MESH)
    pl.semaphore_wait(barrier, len(peers))


class Wires:
    def __init__(self, send_sems, recv_sems):
        self.send_sems, self.recv_sems = send_sems, recv_sems
        self.used = 0
        self.copies = []

    def send(self, source, target, device):
        copy = pltpu.make_async_remote_copy(
            source,
            target,
            self.send_sems.at[self.used],
            self.recv_sems.at[self.used],
            device_id=device,
            device_id_type=MESH,
        )
        copy.start()
        self.used += 1
        self.copies.append(copy)
        return copy

    def finish(self):
        for copy in self.copies:
            copy.wait_send()


def gather_steps(wires, source, place, rows):
    up, down, across = {"seq": seq_at(1, 0)}, {"seq": seq_at(3, 0)}, {"seq": seq_at(0, 1)}
    half = rows // 2
    state = {}

    def first():
        mine = place(lax.axis_index("seq"), 0, rows)
        state["up"] = wires.send(source, mine, up)
        state["down"] = wires.send(source, mine, down)
        state["across"] = wires.send(source, mine, across)

    def second():
        state["up"].wait_recv()
        part = place(seq_at(3, 0), 0, half)
        state["far_up"] = wires.send(part, part, up)
        state["down"].wait_recv()
        part = place(seq_at(1, 0), half, half)
        state["far_down"] = wires.send(part, part, down)
        part = place(seq_at(1, 0), 0, rows)
        state["over"] = wires.send(part, part, across)
        state["across"].wait_recv()
        part = place(seq_at(0, 1), 0, rows)
        state["side_up"] = wires.send(part, part, up)

    def third():
        state["over"].wait_recv()
        part = place(seq_at(1, 1), 0, rows)
        state["side_down"] = wires.send(part, part, down)

    def last():
        for name in ("far_up", "far_down", "side_up", "side_down"):
            state[name].wait_recv()

    return first, second, third, last


GATHER_SENDS = 8


def scatter_steps(wires, parts, inbox):
    up, down, across = {"seq": seq_at(1, 0)}, {"seq": seq_at(3, 0)}, {"seq": seq_at(0, 1)}
    here = lax.axis_index("seq")
    half = parts.shape[1] // 2
    top, bottom = pl.ds(0, half), pl.ds(half, half)
    state = {}

    def first(make):
        make(seq_at(2, 1))
        state["c1"] = wires.send(parts.at[seq_at(2, 1)], inbox.at[0], up)
        make(seq_at(3, 1))
        state["c2"] = wires.send(parts.at[seq_at(3, 1)], inbox.at[1], down)
        far = seq_at(2, 0)
        make(far)
        state["ct"] = wires.send(parts.at[far, top], inbox.at[2, top], down)
        state["cb"] = wires.send(parts.at[far, bottom], inbox.at[2, bottom], up)

    def second():
        state["c1"].wait_recv()
        inbox[0] = inbox[0] + parts[seq_at(1, 1)]
        state["c4"] = wires.send(inbox.at[0], inbox.at[3], across)
        state["c2"].wait_recv()
        inbox[1] = inbox[1] + parts[seq_at(0, 1)]
        state["c5"] = wires.send(inbox.at[1], inbox.at[4], across)
        to = seq_at(3, 0)
        state["c6b"] = wires.send(parts.at[to, bottom], inbox.at[5, bottom], down)
        state["ct"].wait_recv()
        inbox[2, top] = inbox[2, top] + parts[to, top]
        state["c6t"] = wires.send(inbox.at[2, top], inbox.at[5, top], down)

    def third():
        state["cb"].wait_recv()
        state["c4"].wait_recv()
        to = seq_at(1, 0)
        inbox[3] = (parts[to].astype(F32) + inbox[3].astype(F32)).astype(BF16)
        inbox[3, bottom] = inbox[3, bottom] + inbox[2, bottom]
        state["c7"] = wires.send(inbox.at[3], inbox.at[6], up)

    def last():
        for name in ("c5", "c6b", "c6t", "c7"):
            state[name].wait_recv()
        return (parts[here].astype(F32) + inbox[4].astype(F32)) + (
            inbox[5].astype(F32) + inbox[6].astype(F32)
        )

    return first, second, third, last


SCATTER_SENDS = 9


def total_steps(wires, terms, acc, above, below, beside, out):
    core = lax.rem(lax.axis_index("dp"), 2)
    z = lax.rem(lax.axis_index("dp") // 2, 8)
    xh = lax.axis_index("dp") // 16
    twin, up, down = {"dp": dp_at(0, 0, 1)}, {"dp": dp_at(0, 1, 0)}, {"dp": dp_at(0, 7, 0)}
    far = {"dp": dp_at(1, 0, 0)}
    state = {}

    def at(dz):
        return lax.rem(z + dz, 8)

    def start():
        state["twin"] = wires.send(terms.at[:, 1 - core], acc, twin)

    def first():
        state["twin"].wait_recv()
        chips = terms.shape[0]

        @pl.loop(0, chips)
        def _(chip):
            acc[chip] = acc[chip] + terms[chip, core]

        state["u"] = wires.send(acc.at[at(4)], above.at[0, 0], up)
        state["d"] = wires.send(acc.at[8 + at(4)], below.at[0, 1], down)

    def middle(step):
        def run():
            to_up, to_down = at(4 - step), at(4 + step)
            state["u"].wait_recv()
            acc[to_up] = acc[to_up] + above[step - 1, 0]
            if step > 1:
                acc[8 + to_up] = acc[8 + to_up] + above[step - 1, 1]
            state["u0"] = wires.send(acc.at[to_up], above.at[step, 0], up)
            state["u1"] = wires.send(acc.at[8 + to_up], above.at[step, 1], up)
            state["d"].wait_recv()
            acc[8 + to_down] = acc[8 + to_down] + below[step - 1, 1]
            if step > 1:
                acc[to_down] = acc[to_down] + below[step - 1, 0]
            state["d0"] = wires.send(acc.at[to_down], below.at[step, 0], down)
            state["d1"] = wires.send(acc.at[8 + to_down], below.at[step, 1], down)
            state["u"], state["d"] = Both(state["u0"], state["u1"]), Both(state["d0"], state["d1"])

        return run

    def cross():
        state["u"].wait_recv()
        state["d"].wait_recv()
        other = 1 - xh
        to = other * 8 + z
        acc[to] = (
            acc[to].astype(F32) + above[3, other].astype(F32) + below[3, other].astype(F32)
        ).astype(BF16)
        state["far"] = wires.send(acc.at[to], beside, far)

    def last():
        state["far"].wait_recv()
        total = acc[xh * 8 + z].astype(F32) + above[3, xh].astype(F32)
        out[...] = (total + below[3, xh].astype(F32) + beside[...].astype(F32)).astype(BF16)

    return start, first, middle(1), middle(2), middle(3), cross, last


TOTAL_SENDS = 1 + 2 + 3 * 4 + 1


class Both:
    def __init__(self, *copies):
        self.copies = copies

    def wait_recv(self):
        for copy in self.copies:
            copy.wait_recv()


def total_scratch(rows, columns):
    return [
        VMEM((16, rows, columns), BF16),
        VMEM((4, 2, rows, columns), BF16),
        VMEM((4, 2, rows, columns), BF16),
        VMEM((rows, columns), BF16),
    ]


def sems(count):
    return [pltpu.SemaphoreType.DMA((count,)), pltpu.SemaphoreType.DMA((count,))]


def weight_steps(wires, block, blocks):
    core = lax.rem(lax.axis_index("dp"), 2)
    z = lax.rem(lax.axis_index("dp") // 2, 8)
    xh = lax.axis_index("dp") // 16
    twin, up, down = {"dp": dp_at(0, 0, 1)}, {"dp": dp_at(0, 1, 0)}, {"dp": dp_at(0, 7, 0)}
    far = {"dp": dp_at(1, 0, 0)}
    state = {}

    def at(dz):
        return lax.rem(z + dz, 8)

    def start():
        state["far"] = wires.send(block, blocks.at[z, xh, core], far)

    def pass_on(step):
        def run():
            if step == 0:
                state["far"].wait_recv()
            else:
                state["up"].wait_recv()
                state["down"].wait_recv()
            low, high = at(8 - step), at(step)
            if step < 3:
                above, below = blocks.at[low, :, core], blocks.at[high, :, core]
            else:
                above, below = blocks.at[low, 0, core], blocks.at[high, 1, core]
            state["up"] = wires.send(above, above, up)
            state["down"] = wires.send(below, below, down)

        return run

    def share():
        state["up"].wait_recv()
        state["down"].wait_recv()
        part = blocks.at[:, :, core]
        state["twin"] = wires.send(part, part, twin)

    def last():
        state["twin"].wait_recv()

    return start, pass_on(0), pass_on(1), pass_on(2), pass_on(3), share, last


WEIGHT_SENDS = 1 + 8 + 1


def iotas(shape):
    return lax.broadcasted_iota(jnp.int32, shape, 0), lax.broadcasted_iota(jnp.int32, shape, 1)


def one_hot(slot, column, group, slots, offset):
    shift = slots.bit_length() - 1
    device, inside = lax.shift_right_logical(slot, shift), lax.bitwise_and(slot, slots - 1)
    within = jnp.logical_and(inside >= offset, inside < offset + group)
    hit = jnp.logical_and(device * group + inside - offset == column, within)
    return jnp.where(hit, 1.0, 0.0).astype(BF16)


def ring_slot(slot):
    z = lax.shift_right_logical(slot, 7)
    xh = lax.bitwise_and(lax.shift_right_logical(slot, 6), 1)
    return xh * 512 + z * 64 + lax.bitwise_and(slot, 63)


def dot(a, b, dims):
    return lax.dot_general(a, b, (dims, ((), ())), preferred_element_type=F32)


NN, NT, TN = ((1,), (0,)), ((1,), (1,)), ((0,), (0,))


def kernel(
    inputs, saved, attn, upstream, w_qkv, w_out, w_block,
    grad_rows, qkv_sum, out_sum, conv_sum_a, conv_sum_b,
    saved_all, upstream_all, mid_pad, gelu_pad, attn_all, gelu_out_blocks, attn_blocks, slope,
    blocks, normed, proj, expo, sums, grad_attn, query_acc, grad_proj, parts, inbox,
    qkv_terms, out_terms, gelu_wide, w_taps, conv_a, conv_b, gelu_send, gelu_back,
    q0, q1, q2, q3, o0, o1, o2, o3, a0, a1, a2, a3, b0, b1, b2, b3,
    send_sems, recv_sems, own_sems,
):
    here = lax.axis_index("seq")
    core = lax.rem(lax.axis_index("dp"), 2)
    z = lax.rem(lax.axis_index("dp") // 2, 8)
    xh = lax.axis_index("dp") // 16
    rows, channels = saved.shape
    length = 8 * rows
    width = w_out.shape[0]
    half = channels // 2
    scale = HD ** (-0.5)
    meet(
        [{"seq": seq_at(*offset)} for offset in SEQ_OFFSETS]
        + [{"dp": dp_at(*offset)} for offset in ((0, 0, 1), (0, 1, 0), (0, 7, 0), (1, 0, 0))]
    )
    wires = Wires(send_sems, recv_sems)

    def span(s, start=0, count=rows, base=0):
        return pl.ds(pl.multiple_of(s * rows + (base + start), 32), count)

    def place_of(ref, base=0):
        return lambda s, start, count: ref.at[span(s, start, count, base)]

    get_saved = gather_steps(wires, saved, place_of(saved_all), rows)
    get_upstream = gather_steps(wires, upstream, place_of(upstream_all), rows)
    get_weight = weight_steps(wires, w_block, blocks)
    get_saved[0]()
    get_weight[0]()
    kept = [
        pltpu.make_async_copy(saved, saved_all.at[span(here)], own_sems.at[0]),
        pltpu.make_async_copy(upstream, upstream_all.at[span(here)], own_sems.at[1]),
        pltpu.make_async_copy(w_block, blocks.at[z, xh, core], own_sems.at[2]),
    ]
    for copy in kept:
        copy.start()

    pair = 2 * width
    row_of, column_of = iotas((pair, width))
    picks = [(row_of == column_of + part * width) for part in range(2)]
    picks = [jnp.where(pick, 1.0, 0.0).astype(BF16) for pick in picks]
    for index in range(4):
        columns = pl.ds(index * pair, pair)
        value = inputs[:, columns].astype(F32)
        cubic = value * value * 0.044715
        inner = math.sqrt(2.0 / math.pi) * value * (1.0 + cubic)
        bend = jnp.tanh(inner)
        gelu = (0.5 * value * (1.0 + bend)).astype(BF16)
        slope[:, columns] = 0.5 * (1.0 + bend) + 0.5 * value * (1.0 - bend * bend) * (
            math.sqrt(2.0 / math.pi) * (1.0 + 3.0 * cubic)
        )
        attn_pair = attn[:, columns]
        for part in range(2):
            gelu_out_blocks[2 * index + part] = dot(gelu, picks[part], NN).astype(BF16)
            attn_blocks[2 * index + part] = dot(attn_pair, picks[part], NN).astype(BF16)
    zeros = jnp.zeros((REACH, channels), BF16)
    mid_pad[pl.ds(0, REACH)] = zeros
    mid_pad[pl.ds(REACH + length, REACH)] = zeros
    gelu_pad[pl.ds(0, REACH)] = zeros[:, :width]
    gelu_pad[pl.ds(REACH + length, REACH)] = zeros[:, :width]
    for copy in kept:
        copy.wait()

    def project(s):
        at = span(s)
        wide = saved_all[at].astype(F32)
        inverse = lax.rsqrt(jnp.mean(wide * wide, axis=-1, keepdims=True) + EPSILON)
        block = (wide * inverse).astype(BF16)
        normed[at] = block
        for j in range(3):
            proj[j, at] = dot(block, w_qkv[j], NT).astype(BF16)

    def project_all(offsets):
        for offset in offsets:
            project(seq_at(*offset))

    project_all([(0, 0)])
    get_saved[1]()
    get_upstream[0]()
    get_weight[1]()
    project_all([(3, 0), (1, 0), (0, 1)])
    get_saved[2]()
    get_weight[2]()
    project_all([(1, 1)])
    get_saved[3]()
    get_weight[3]()
    project_all([(2, 0), (3, 1), (2, 1)])
    get_upstream[1]()
    swapped = []
    for offset in SEQ_OFFSETS:
        to = seq_at(*offset)
        swapped.append(wires.send(attn_blocks.at[to], attn_all.at[span(here)], {"seq": to}))
        swapped.append(
            wires.send(gelu_out_blocks.at[to], gelu_pad.at[span(here, base=REACH)], {"seq": to})
        )
    attn_all[span(here)] = attn_blocks[here]
    gelu_pad[span(here, base=REACH)] = gelu_out_blocks[here]
    get_weight[4]()

    tile = 256
    sums[...] = jnp.zeros_like(sums)

    @pl.loop(0, length // tile)
    def _(index):
        at = pl.ds(pl.multiple_of(index * tile, tile), tile)
        weight = jnp.exp(dot(proj[1, at], proj[0], NT) * scale)
        expo[at] = weight
        sums[...] += jnp.sum(weight, axis=0, keepdims=True)

    def attend(s):
        at = span(s)
        grad_attn[at] = dot(upstream_all[at], w_out[...], NT).astype(BF16)

    def attend_all(offsets):
        for offset in offsets:
            attend(seq_at(*offset))

    attend_all([(0, 0), (3, 0), (1, 0), (0, 1)])
    get_upstream[2]()
    get_weight[5]()
    attend_all([(1, 1)])
    get_upstream[3]()
    attend_all([(2, 0), (3, 1), (2, 1)])
    for copy in swapped:
        copy.wait_recv()

    product = grad_attn[...].astype(F32) * attn_all[...].astype(F32)
    delta = lax.dot_general(
        jnp.ones((8, width), F32), product, (NT, ((), ())),
        precision=lax.Precision.HIGHEST, preferred_element_type=F32,
    )[0:1]
    ratio = 1.0 / sums[...]
    query_acc[...] = jnp.zeros_like(query_acc)

    @pl.loop(0, length // tile)
    def _(index):
        at = pl.ds(pl.multiple_of(index * tile, tile), tile)
        probs = expo[at] * ratio
        grad_prob = dot(proj[2, at], grad_attn[...], NT)
        score = (probs * (grad_prob - delta) * scale).astype(BF16)
        grad_proj[1, at] = dot(score, proj[0], NN).astype(BF16)
        grad_proj[2, at] = dot(probs.astype(BF16), grad_attn[...], NN).astype(BF16)
        query_acc[...] += dot(score, proj[1, at], TN)

    grad_proj[0] = query_acc[...].astype(BF16)

    def acts(s):
        at = span(s)

        @pl.loop(0, channels // 512)
        def _(index):
            columns = pl.ds(pl.multiple_of(index * 512, 512), 512)
            total = dot(grad_proj[0, at], w_qkv[0, :, columns], NN)
            total += dot(grad_proj[1, at], w_qkv[1, :, columns], NN)
            total += dot(grad_proj[2, at], w_qkv[2, :, columns], NN)
            parts[s, :, columns] = total.astype(BF16)

    scatter = scatter_steps(wires, parts, inbox)
    scatter[0](acts)
    for offset in ((1, 1), (0, 1), (3, 0), (1, 0), (0, 0)):
        acts(seq_at(*offset))

    sum_qkv = total_steps(wires, qkv_terms, q0, q1, q2, q3, qkv_sum)
    sum_out = total_steps(wires, out_terms, o0, o1, o2, o3, out_sum)

    @pl.loop(0, 4)
    def _(index):
        columns = pl.ds(pl.multiple_of(index * 384, 384), 384)
        turned = normed[:, columns].T
        for j in range(3):
            result = dot(turned, grad_proj[j], NN).astype(BF16)
            qkv_terms[pl.ds(index * 4, 4), :, pl.ds(j * 48, 48)] = result.reshape(4, 2, 48, width)

    sum_qkv[0]()
    scatter[1]()
    slot_of, column_of = iotas((512, width))
    for part in range(2):
        pick = one_hot(slot_of, column_of, 6, 16, 6 * part)
        gelu_wide[pl.ds(512 * part, 512)] = dot(pick, attn_all[...], NT).astype(BF16)

    @pl.loop(0, 3)
    def _(index):
        first = dot(gelu_wide[pl.ds(0, 512)], upstream_all[:, pl.ds(pl.multiple_of(index * 256, 256), 256)], NN)
        second = dot(
            gelu_wide[pl.ds(512, 512)], upstream_all[:, pl.ds(pl.multiple_of(half + index * 256, 256), 256)], NN
        )
        result = (first + second).astype(BF16).reshape(16, 2, 16, 256)
        out_terms[:, :, :, pl.ds(pl.multiple_of(index * 256, 256), 256)] = result

    sum_out[0]()
    sum_qkv[1]()
    scatter[2]()
    sum_out[1]()

    slot_of, column_of = iotas((tile, width))

    @pl.loop(0, 4)
    def _(index):
        total = jnp.zeros((tile, length), F32)
        for tap in range(TAPS):
            pick = one_hot(slot_of + index * tile, column_of, 6, 32, 6 * tap)
            total += dot(pick, gelu_pad[pl.ds(DILATION * tap, length)], NT)
        gelu_wide[pl.ds(pl.multiple_of(index * tile, tile), tile)] = total.astype(BF16)

    sum_qkv[2]()
    sum_out[2]()
    acts_here = scatter[3]()
    wide = saved[...].astype(F32)
    inverse = lax.rsqrt(jnp.mean(wide * wide, axis=-1, keepdims=True) + EPSILON)
    straight = wide * inverse
    grad = inverse * (
        acts_here - straight * jnp.mean(acts_here * straight, axis=-1, keepdims=True)
    )
    at_mine = span(here, base=REACH)
    mid_pad[at_mine] = (upstream[...].astype(F32) + grad).astype(BF16)
    get_mid = gather_steps(wires, mid_pad.at[at_mine], place_of(mid_pad, REACH), rows)
    get_mid[0]()
    sum_qkv[3]()
    sum_out[3]()

    get_weight[6]()
    row_of, slot_of = iotas((width, length))

    for tap in range(TAPS):
        pick = one_hot(ring_slot(slot_of), row_of, 6, 32, 6 * tap)

        @pl.loop(0, 3)
        def _(index):
            columns = pl.ds(pl.multiple_of(index * 512, 512), 512)
            weight = blocks[:, :, :, :, columns].reshape(length, 512)
            w_taps[tap, :, columns] = dot(pick, weight, NN).astype(BF16)

    get_mid[1]()
    sum_qkv[4]()
    sum_out[4]()
    get_mid[2]()
    sum_qkv[5]()
    sum_out[5]()
    sum_qkv[6]()
    sum_out[6]()
    get_mid[3]()

    totals = [
        total_steps(wires, conv_a, a0, a1, a2, a3, conv_sum_a),
        total_steps(wires, conv_b, b0, b1, b2, b3, conv_sum_b),
    ]
    for part, terms in enumerate((conv_a, conv_b)):

        @pl.loop(0, 4)
        def _(index):
            at = pl.ds(pl.multiple_of(index * tile, tile), tile)
            for column in range(0, half, 256):
                result = dot(
                    gelu_wide[at],
                    mid_pad[pl.ds(REACH, length), pl.ds(part * half + column, 256)],
                    NN,
                ).astype(BF16)
                terms[pl.ds(index * 4, 4), :, :, pl.ds(column, 256)] = result.reshape(4, 2, 32, 256)

        totals[part][0]()

    @pl.loop(0, length // tile)
    def _(index):
        total = jnp.zeros((tile, width), F32)
        for tap in range(TAPS):
            at = pl.ds(pl.multiple_of(index * tile + (2 * REACH - DILATION * tap), 32), tile)
            total += dot(mid_pad[at], w_taps[tap], NT)
        gelu_send[pl.ds(index * 2, 2)] = total.astype(BF16).reshape(2, rows, width)

    for steps in totals:
        steps[1]()
    swapped = []
    for offset in SEQ_OFFSETS:
        to = seq_at(*offset)
        swapped.append(wires.send(gelu_send.at[to], gelu_back.at[here], {"seq": to}))
    gelu_back[here] = gelu_send[here]
    for step in range(2, 5):
        for steps in totals:
            steps[step]()
    for copy in swapped:
        copy.wait_recv()
    for index in range(4):
        columns = pl.ds(index * pair, pair)
        gelu_grad = dot(gelu_back[2 * index], picks[0], NT) + dot(
            gelu_back[2 * index + 1], picks[1], NT
        )
        grad_rows[:, columns] = (
            mid_pad[at_mine, columns].astype(F32) + slope[:, columns] * gelu_grad
        ).astype(BF16)
    for step in range(5, 7):
        for steps in totals:
            steps[step]()
    wires.finish()


def run(inputs, saved, attn, upstream, w_qkv, w_out, w_block):
    rows, channels = saved.shape
    length, width, half = 8 * rows, w_out.shape[0], channels // 2
    count = 3 * GATHER_SENDS + SCATTER_SENDS + WEIGHT_SENDS + 3 * 7 + 4 * TOTAL_SENDS
    in_vmem = pl.BlockSpec(memory_space=VMEM)
    return pl.pallas_call(
        kernel,
        out_shape=[
            jax.ShapeDtypeStruct((rows, channels), BF16),
            jax.ShapeDtypeStruct((144, width), BF16),
            jax.ShapeDtypeStruct((16, half), BF16),
            jax.ShapeDtypeStruct((32, half), BF16),
            jax.ShapeDtypeStruct((32, half), BF16),
        ],
        in_specs=[in_vmem] * 7,
        out_specs=[in_vmem] * 5,
        scratch_shapes=[
            VMEM((length, channels), BF16),
            VMEM((length, channels), BF16),
            VMEM((length + 2 * REACH, channels), BF16),
            VMEM((length + 2 * REACH, width), BF16),
            VMEM((length, width), BF16),
            VMEM((8, rows, width), BF16),
            VMEM((8, rows, width), BF16),
            VMEM((rows, channels), F32),
            VMEM((8, 2, 2, 32, channels), BF16),
            VMEM((length, channels), BF16),
            VMEM((3, length, width), BF16),
            VMEM((length, length), F32),
            VMEM((1, length), F32),
            VMEM((length, width), BF16),
            VMEM((length, width), F32),
            VMEM((3, length, width), BF16),
            VMEM((8, rows, channels), BF16),
            VMEM((7, rows, channels), BF16),
            VMEM((16, 2, 144, width), BF16),
            VMEM((16, 2, 16, half), BF16),
            VMEM((length, length), BF16),
            VMEM((TAPS, width, channels), BF16),
            VMEM((16, 2, 32, half), BF16),
            VMEM((16, 2, 32, half), BF16),
            VMEM((8, rows, width), BF16),
            VMEM((8, rows, width), BF16),
        ]
        + total_scratch(144, width)
        + total_scratch(16, half)
        + total_scratch(32, half)
        + total_scratch(32, half)
        + sems(count)
        + [pltpu.SemaphoreType.DMA((3,))],
        compiler_params=pltpu.CompilerParams(
            collective_id=1, has_side_effects=True, vmem_limit_bytes=58 << 20
        ),
    )(inputs, saved, attn, upstream, w_qkv, w_out, w_block)


def local(inputs, saved, attn_saved, upstream, w_qkv, w_out, w_conv):
    channels = inputs.shape[2]
    width = w_out.shape[0]
    taps_rows = w_conv.shape[0] * w_conv.shape[1]
    w_block = jnp.pad(w_conv.reshape(taps_rows, channels), ((0, 32 - taps_rows), (0, 0)))
    grad_rows, qkv_sum, out_sum, sum_a, sum_b = run(
        inputs[0], saved[0], attn_saved[0], upstream[0], w_qkv.transpose(1, 2, 0), w_out, w_block
    )
    out_pair = out_sum[:12].reshape(2, 6, channels // 2)
    return (
        grad_rows[None],
        qkv_sum.reshape(3, channels // 32, width).transpose(1, 0, 2),
        jnp.concatenate([out_pair[0], out_pair[1]], axis=1),
        jnp.concatenate([sum_a, sum_b], axis=1)[:taps_rows].reshape(w_conv.shape),
    )


def solution(mesh):
    placed = (
        P("dp", "seq", None),
        P("dp", "seq", None),
        P("dp", "seq", None),
        P("dp", "seq", None),
        P(None, None, "seq"),
        P("seq", None),
        P(None, ("seq", "dp"), None),
    )
    return jax.shard_map(
        local,
        mesh=mesh,
        in_specs=placed,
        out_specs=(
            P("dp", "seq", None),
            P("dp", None, "seq"),
            P(("seq", "dp"), None),
            P(None, ("seq", "dp"), None),
        ),
        check_vma=False,
    )
```

profile of v0, /device:TPU:8, one launch (start us, length us, event | category | flops | bytes accessed | tf_op | source)
XLA Modules:
  0.0 173.7 jit_solution(4393915285367215635)
XLA Ops:
  0.6 0.9 reshape.22
  1.6 0.7 pad.4.w_block
  2.2 165.2 %shard_map.102 = (bf16[128,1536]{1,0:T(8,128)(2,1)}, bf16[144,192]{1,0:T(8,128)(2,1)}, bf16[16,768]{1,0:T(8,128)(2,1)}, bf16[32,768]{1,0:T(8,128)(2,1)}, bf16[32,768]{1,0:T(8,128)(2,1)}) custom-call(bf16[128,1536]{1,0:T(8,128)(2,1)} %bitcast.11, bf16[128,1536]{1,0:T(8,128)(2,1)} %bitcast.12, bf16[128,1536]{1,0:T(8,128)(2,1)} %bitcast.13, ...), custom_call_target="tpu_custom_call" | custom-call | tf_op jit(solution)/shard_map/pallas_call | solution.py:624
  167.4 0.8 fusion
  168.3 0.6 pad_maximum_fusion.1
  168.9 0.8 pad_maximum_fusion
  169.7 0.7 reshape.24
  170.4 1.8 %copy.13 = bf16[1,128,1536]{2,1,0:T(8,128)(2,1)} copy(bf16[1,128,1536]{2,1,0:T(8,128)(2,1)} %bitcast.10) | data formatting | bytes 786432
  172.2 1.5 copy.14
where the time goes:
time: 176 us; the launch traced here: 174 us
  Pallas kernels  165 us (94%)
  local copies, waits for them, and re-layouts  6.38 us (4%)
    pallas_call x1, Pallas kernels, run(): pl.pallas_call(kernel, out_shape=[jax.ShapeDtypeStruct((rows, channels),...  165 us

commit v1 on v0

--- a/solution.py
+++ b/solution.py
@@ -67,7 +67,10 @@
             copy.wait_send()
 
 
-def gather_steps(wires, source, place, rows):
+def gather_steps(wires, source, whole, base, rows):
+    def place(s, start, count):
+        return whole(s, base + start, count)
+
     up, down, across = {"seq": seq_at(1, 0)}, {"seq": seq_at(3, 0)}, {"seq": seq_at(0, 1)}
     half = rows // 2
     state = {}
@@ -106,52 +109,59 @@
 GATHER_SENDS = 8
 
 
-def scatter_steps(wires, parts, inbox):
+def scatter_steps(wires, parts, inbox, base, rows):
     up, down, across = {"seq": seq_at(1, 0)}, {"seq": seq_at(3, 0)}, {"seq": seq_at(0, 1)}
     here = lax.axis_index("seq")
-    half = parts.shape[1] // 2
-    top, bottom = pl.ds(0, half), pl.ds(half, half)
+    every = pl.ds(base, rows)
+    top, bottom = pl.ds(base, rows // 2), pl.ds(base + rows // 2, rows // 2)
     state = {}
 
-    def first(make):
-        make(seq_at(2, 1))
-        state["c1"] = wires.send(parts.at[seq_at(2, 1)], inbox.at[0], up)
-        make(seq_at(3, 1))
-        state["c2"] = wires.send(parts.at[seq_at(3, 1)], inbox.at[1], down)
-        far = seq_at(2, 0)
-        make(far)
-        state["ct"] = wires.send(parts.at[far, top], inbox.at[2, top], down)
-        state["cb"] = wires.send(parts.at[far, bottom], inbox.at[2, bottom], up)
-
-    def second():
+    def post(name, source, target, device):
+        state[name] = wires.send(source, target, device)
+
+    def far_side_up():
+        post("c1", parts.at[seq_at(2, 1), every], inbox.at[0, every], up)
+
+    def far_side_down():
+        post("c2", parts.at[seq_at(3, 1), every], inbox.at[1, every], down)
+
+    def far():
+        post("ct", parts.at[seq_at(2, 0), top], inbox.at[2, top], down)
+        post("cb", parts.at[seq_at(2, 0), bottom], inbox.at[2, bottom], up)
+
+    def across_first():
         state["c1"].wait_recv()
-        inbox[0] = inbox[0] + parts[seq_at(1, 1)]
-        state["c4"] = wires.send(inbox.at[0], inbox.at[3], across)
+        inbox[0, every] = inbox[0, every] + parts[seq_at(1, 1), every]
+        post("c4", inbox.at[0, every], inbox.at[3, every], across)
+
+    def across_second():
         state["c2"].wait_recv()
-        inbox[1] = inbox[1] + parts[seq_at(0, 1)]
-        state["c5"] = wires.send(inbox.at[1], inbox.at[4], across)
+        inbox[1, every] = inbox[1, every] + parts[seq_at(0, 1), every]
+        post("c5", inbox.at[1, every], inbox.at[4, every], across)
+
+    def near_down():
         to = seq_at(3, 0)
-        state["c6b"] = wires.send(parts.at[to, bottom], inbox.at[5, bottom], down)
+        post("c6b", parts.at[to, bottom], inbox.at[5, bottom], down)
         state["ct"].wait_recv()
         inbox[2, top] = inbox[2, top] + parts[to, top]
-        state["c6t"] = wires.send(inbox.at[2, top], inbox.at[5, top], down)
-
-    def third():
+        post("c6t", inbox.at[2, top], inbox.at[5, top], down)
+
+    def near_up():
         state["cb"].wait_recv()
         state["c4"].wait_recv()
         to = seq_at(1, 0)
-        inbox[3] = (parts[to].astype(F32) + inbox[3].astype(F32)).astype(BF16)
+        inbox[3, every] = (parts[to, every].astype(F32) + inbox[3, every].astype(F32)).astype(BF16)
         inbox[3, bottom] = inbox[3, bottom] + inbox[2, bottom]
-        state["c7"] = wires.send(inbox.at[3], inbox.at[6], up)
+        post("c7", inbox.at[3, every], inbox.at[6, every], up)
 
     def last():
         for name in ("c5", "c6b", "c6t", "c7"):
             state[name].wait_recv()
-        return (parts[here].astype(F32) + inbox[4].astype(F32)) + (
-            inbox[5].astype(F32) + inbox[6].astype(F32)
+        return (parts[here, every].astype(F32) + inbox[4, every].astype(F32)) + (
+            inbox[5, every].astype(F32) + inbox[6, every].astype(F32)
         )
 
-    return first, second, third, last
+    return far_side_up, far_side_down, far, across_first, across_second, near_down, near_up, last
 
 
 SCATTER_SENDS = 9
@@ -345,10 +355,23 @@
     def place_of(ref, base=0):
         return lambda s, start, count: ref.at[span(s, start, count, base)]
 
-    get_saved = gather_steps(wires, saved, place_of(saved_all), rows)
-    get_upstream = gather_steps(wires, upstream, place_of(upstream_all), rows)
+    half_rows = rows // 2
+
+    def halves(source, whole):
+        return [
+            gather_steps(wires, source(part * half_rows), whole, part * half_rows, half_rows)
+            for part in range(2)
+        ]
+
+    def rows_of(ref):
+        return lambda start: ref.at[pl.ds(start, half_rows)]
+
+    get_saved = halves(rows_of(saved), place_of(saved_all))
+    get_upstream = halves(rows_of(upstream), place_of(upstream_all))
+    get_mid = halves(lambda start: mid_pad.at[span(here, start, half_rows, REACH)], place_of(mid_pad, REACH))
     get_weight = weight_steps(wires, w_block, blocks)
-    get_saved[0]()
+    get_saved[0][0]()
+    get_saved[1][0]()
     get_weight[0]()
     kept = [
         pltpu.make_async_copy(saved, saved_all.at[span(here)], own_sems.at[0]),
@@ -393,31 +416,38 @@
         for j in range(3):
             proj[j, at] = dot(block, w_qkv[j], NT).astype(BF16)
 
-    def project_all(offsets):
+    def project_all(*offsets):
         for offset in offsets:
             project(seq_at(*offset))
 
-    project_all([(0, 0)])
-    get_saved[1]()
-    get_upstream[0]()
+    get_saved[0][1]()
+    project_all((0, 0))
+    get_saved[1][1]()
+    get_upstream[0][0]()
+    get_upstream[1][0]()
     get_weight[1]()
-    project_all([(3, 0), (1, 0), (0, 1)])
-    get_saved[2]()
+    project_all((3, 0))
+    get_saved[0][2]()
+    project_all((1, 0))
+    get_saved[1][2]()
     get_weight[2]()
-    project_all([(1, 1)])
-    get_saved[3]()
+    project_all((0, 1))
+    get_upstream[0][1]()
+    get_saved[0][3]()
+    get_saved[1][3]()
+    project_all((1, 1))
+    get_upstream[1][1]()
     get_weight[3]()
-    project_all([(2, 0), (3, 1), (2, 1)])
-    get_upstream[1]()
     swapped = []
     for offset in SEQ_OFFSETS:
         to = seq_at(*offset)
         swapped.append(wires.send(attn_blocks.at[to], attn_all.at[span(here)], {"seq": to}))
-        swapped.append(
-            wires.send(gelu_out_blocks.at[to], gelu_pad.at[span(here, base=REACH)], {"seq": to})
-        )
     attn_all[span(here)] = attn_blocks[here]
     gelu_pad[span(here, base=REACH)] = gelu_out_blocks[here]
+    project_all((2, 0), (3, 1))
+    get_upstream[0][2]()
+    project_all((2, 1))
+    get_upstream[1][2]()
     get_weight[4]()
 
     tile = 256
@@ -434,16 +464,21 @@
         at = span(s)
         grad_attn[at] = dot(upstream_all[at], w_out[...], NT).astype(BF16)
 
-    def attend_all(offsets):
+    def attend_all(*offsets):
         for offset in offsets:
             attend(seq_at(*offset))
 
-    attend_all([(0, 0), (3, 0), (1, 0), (0, 1)])
-    get_upstream[2]()
+    attend_all((0, 0), (3, 0), (1, 0), (0, 1))
     get_weight[5]()
-    attend_all([(1, 1)])
-    get_upstream[3]()
-    attend_all([(2, 0), (3, 1), (2, 1)])
+    get_upstream[0][3]()
+    get_upstream[1][3]()
+    attend_all((1, 1), (2, 0), (3, 1), (2, 1))
+    gelu_swapped = []
+    for offset in SEQ_OFFSETS:
+        to = seq_at(*offset)
+        gelu_swapped.append(
+            wires.send(gelu_out_blocks.at[to], gelu_pad.at[span(here, base=REACH)], {"seq": to})
+        )
     for copy in swapped:
         copy.wait_recv()
 
@@ -478,24 +513,46 @@
             total += dot(grad_proj[2, at], w_qkv[2, :, columns], NN)
             parts[s, :, columns] = total.astype(BF16)
 
-    scatter = scatter_steps(wires, parts, inbox)
-    scatter[0](acts)
-    for offset in ((1, 1), (0, 1), (3, 0), (1, 0), (0, 0)):
-        acts(seq_at(*offset))
+    scatter = [scatter_steps(wires, parts, inbox, part * half_rows, half_rows) for part in range(2)]
+
+    def both(step):
+        for steps in scatter:
+            steps[step]()
+
+    acts(seq_at(2, 1))
+    both(0)
+    acts(seq_at(3, 1))
+    both(1)
+    acts(seq_at(2, 0))
+    both(2)
+    acts(seq_at(1, 1))
+    acts(seq_at(0, 1))
+    both(3)
+    acts(seq_at(3, 0))
+    acts(seq_at(1, 0))
+    both(4)
+    acts(seq_at(0, 0))
+    both(5)
 
     sum_qkv = total_steps(wires, qkv_terms, q0, q1, q2, q3, qkv_sum)
     sum_out = total_steps(wires, out_terms, o0, o1, o2, o3, out_sum)
 
-    @pl.loop(0, 4)
-    def _(index):
-        columns = pl.ds(pl.multiple_of(index * 384, 384), 384)
-        turned = normed[:, columns].T
-        for j in range(3):
-            result = dot(turned, grad_proj[j], NN).astype(BF16)
-            qkv_terms[pl.ds(index * 4, 4), :, pl.ds(j * 48, 48)] = result.reshape(4, 2, 48, width)
-
+    def seq_qkv(first):
+        @pl.loop(first, first + 2)
+        def _(index):
+            columns = pl.ds(pl.multiple_of(index * 384, 384), 384)
+            turned = normed[:, columns].T
+            for j in range(3):
+                result = dot(turned, grad_proj[j], NN).astype(BF16)
+                qkv_terms[pl.ds(index * 4, 4), :, pl.ds(j * 48, 48)] = result.reshape(
+                    4, 2, 48, width
+                )
+
+    seq_qkv(0)
+    scatter[0][6]()
+    seq_qkv(2)
+    scatter[1][6]()
     sum_qkv[0]()
-    scatter[1]()
     slot_of, column_of = iotas((512, width))
     for part in range(2):
         pick = one_hot(slot_of, column_of, 6, 16, 6 * part)
@@ -503,18 +560,41 @@
 
     @pl.loop(0, 3)
     def _(index):
-        first = dot(gelu_wide[pl.ds(0, 512)], upstream_all[:, pl.ds(pl.multiple_of(index * 256, 256), 256)], NN)
+        first = dot(
+            gelu_wide[pl.ds(0, 512)],
+            upstream_all[:, pl.ds(pl.multiple_of(index * 256, 256), 256)],
+            NN,
+        )
         second = dot(
-            gelu_wide[pl.ds(512, 512)], upstream_all[:, pl.ds(pl.multiple_of(half + index * 256, 256), 256)], NN
+            gelu_wide[pl.ds(512, 512)],
+            upstream_all[:, pl.ds(pl.multiple_of(half + index * 256, 256), 256)],
+            NN,
         )
         result = (first + second).astype(BF16).reshape(16, 2, 16, 256)
         out_terms[:, :, :, pl.ds(pl.multiple_of(index * 256, 256), 256)] = result
 
     sum_out[0]()
     sum_qkv[1]()
-    scatter[2]()
+    at_mine = span(here, base=REACH)
+    for part in range(2):
+        acts_here = scatter[part][7]()
+        at = pl.ds(part * half_rows, half_rows)
+        wide = saved[at].astype(F32)
+        inverse = lax.rsqrt(jnp.mean(wide * wide, axis=-1, keepdims=True) + EPSILON)
+        straight = wide * inverse
+        grad = inverse * (
+            acts_here - straight * jnp.mean(acts_here * straight, axis=-1, keepdims=True)
+        )
+        mid_pad[span(here, part * half_rows, half_rows, REACH)] = (
+            upstream[at].astype(F32) + grad
+        ).astype(BF16)
+        get_mid[part][0]()
     sum_out[1]()
-
+    sum_qkv[2]()
+    sum_out[2]()
+
+    for copy in gelu_swapped:
+        copy.wait_recv()
     slot_of, column_of = iotas((tile, width))
 
     @pl.loop(0, 4)
@@ -525,43 +605,35 @@
             total += dot(pick, gelu_pad[pl.ds(DILATION * tap, length)], NT)
         gelu_wide[pl.ds(pl.multiple_of(index * tile, tile), tile)] = total.astype(BF16)
 
-    sum_qkv[2]()
-    sum_out[2]()
-    acts_here = scatter[3]()
-    wide = saved[...].astype(F32)
-    inverse = lax.rsqrt(jnp.mean(wide * wide, axis=-1, keepdims=True) + EPSILON)
-    straight = wide * inverse
-    grad = inverse * (
-        acts_here - straight * jnp.mean(acts_here * straight, axis=-1, keepdims=True)
-    )
-    at_mine = span(here, base=REACH)
-    mid_pad[at_mine] = (upstream[...].astype(F32) + grad).astype(BF16)
-    get_mid = gather_steps(wires, mid_pad.at[at_mine], place_of(mid_pad, REACH), rows)
-    get_mid[0]()
+    get_mid[0][1]()
+    get_mid[1][1]()
     sum_qkv[3]()
     sum_out[3]()
 
     get_weight[6]()
     row_of, slot_of = iotas((width, length))
 
-    for tap in range(TAPS):
-        pick = one_hot(ring_slot(slot_of), row_of, 6, 32, 6 * tap)
-
-        @pl.loop(0, 3)
-        def _(index):
-            columns = pl.ds(pl.multiple_of(index * 512, 512), 512)
-            weight = blocks[:, :, :, :, columns].reshape(length, 512)
-            w_taps[tap, :, columns] = dot(pick, weight, NN).astype(BF16)
-
-    get_mid[1]()
+    def taps_of(first, last):
+        for tap in range(first, last):
+            pick = one_hot(ring_slot(slot_of), row_of, 6, 32, 6 * tap)
+
+            @pl.loop(0, 3)
+            def _(index):
+                columns = pl.ds(pl.multiple_of(index * 512, 512), 512)
+                weight = blocks[:, :, :, :, columns].reshape(length, 512)
+                w_taps[tap, :, columns] = dot(pick, weight, NN).astype(BF16)
+
+    taps_of(0, 3)
+    get_mid[0][2]()
     sum_qkv[4]()
     sum_out[4]()
-    get_mid[2]()
-    sum_qkv[5]()
-    sum_out[5]()
-    sum_qkv[6]()
-    sum_out[6]()
-    get_mid[3]()
+    taps_of(3, TAPS)
+    get_mid[1][2]()
+    for step in (5, 6):
+        sum_qkv[step]()
+        sum_out[step]()
+    get_mid[0][3]()
+    get_mid[1][3]()
 
     totals = [
         total_steps(wires, conv_a, a0, a1, a2, a3, conv_sum_a),
@@ -582,22 +654,27 @@
 
         totals[part][0]()
 
-    @pl.loop(0, length // tile)
-    def _(index):
-        total = jnp.zeros((tile, width), F32)
-        for tap in range(TAPS):
-            at = pl.ds(pl.multiple_of(index * tile + (2 * REACH - DILATION * tap), 32), tile)
-            total += dot(mid_pad[at], w_taps[tap], NT)
-        gelu_send[pl.ds(index * 2, 2)] = total.astype(BF16).reshape(2, rows, width)
-
-    for steps in totals:
-        steps[1]()
+    def grad_gelu(first):
+        @pl.loop(first, first + 2)
+        def _(index):
+            total = jnp.zeros((tile, width), F32)
+            for tap in range(TAPS):
+                at = pl.ds(pl.multiple_of(index * tile + (2 * REACH - DILATION * tap), 32), tile)
+                total += dot(mid_pad[at], w_taps[tap], NT)
+            gelu_send[pl.ds(index * 2, 2)] = total.astype(BF16).reshape(2, rows, width)
+
+    totals[0][1]()
+    grad_gelu(0)
+    totals[1][1]()
+    totals[0][2]()
+    grad_gelu(2)
+    totals[1][2]()
     swapped = []
     for offset in SEQ_OFFSETS:
         to = seq_at(*offset)
         swapped.append(wires.send(gelu_send.at[to], gelu_back.at[here], {"seq": to}))
     gelu_back[here] = gelu_send[here]
-    for step in range(2, 5):
+    for step in range(3, 5):
         for steps in totals:
             steps[step]()
     for copy in swapped:
@@ -619,7 +696,7 @@
 def run(inputs, saved, attn, upstream, w_qkv, w_out, w_block):
     rows, channels = saved.shape
     length, width, half = 8 * rows, w_out.shape[0], channels // 2
-    count = 3 * GATHER_SENDS + SCATTER_SENDS + WEIGHT_SENDS + 3 * 7 + 4 * TOTAL_SENDS
+    count = 2 * (3 * GATHER_SENDS + SCATTER_SENDS) + WEIGHT_SENDS + 3 * 7 + 4 * TOTAL_SENDS
     in_vmem = pl.BlockSpec(memory_space=VMEM)
     return pl.pallas_call(
         kernel,

time: 176 us -> 155 us (0.88); the launches traced: 174 us -> 154 us
  Pallas kernels: 165 us -> 146 us
    pallas_call x1, Pallas kernels: 165 us -> 146 us  [run(): pl.pallas_call(kernel, out_shape=[jax.ShapeDtypeStruct((rows, channels),...]
where the time goes in v1:
time: 155 us; the launch traced here: 154 us
  Pallas kernels  146 us (94%)
  local copies, waits for them, and re-layouts  6.38 us (4%)
    pallas_call x1, Pallas kernels, run(): pl.pallas_call(kernel, out_shape=[jax.ShapeDtypeStruct((rows, channels),...  146 us
    unnamed x2, local copies, waits for them, and re-layouts  3.29 us

profile of v1, /device:TPU:8, one launch (start us, length us, event | category | flops | bytes accessed | tf_op | source)
XLA Modules:
  0.0 154.4 jit_solution(4623969107505033684)
XLA Ops:
  0.6 0.9 reshape.22
  1.6 0.7 pad.4.w_block
  2.2 146.0 %shard_map.102 = (bf16[128,1536]{1,0:T(8,128)(2,1)}, bf16[144,192]{1,0:T(8,128)(2,1)}, bf16[16,768]{1,0:T(8,128)(2,1)}, bf16[32,768]{1,0:T(8,128)(2,1)}, bf16[32,768]{1,0:T(8,128)(2,1)}) custom-call(bf16[128,1536]{1,0:T(8,128)(2,1)} %bitcast.11, bf16[128,1536]{1,0:T(8,128)(2,1)} %bitcast.12, bf16[128,1536]{1,0:T(8,128)(2,1)} %bitcast.13, ...), custom_call_target="tpu_custom_call" | custom-call | tf_op jit(solution)/shard_map/pallas_call | solution.py:701
  148.2 0.8 fusion
  149.0 0.6 pad_maximum_fusion.1
  149.6 0.8 pad_maximum_fusion
  150.5 0.7 reshape.24
  151.2 1.8 %copy.13 = bf16[1,128,1536]{2,1,0:T(8,128)(2,1)} copy(bf16[1,128,1536]{2,1,0:T(8,128)(2,1)} %bitcast.10) | data formatting | bytes 786432
  152.9 1.5 copy.14

commit v2 on v1

--- a/solution.py
+++ b/solution.py
@@ -167,7 +167,7 @@
 SCATTER_SENDS = 9
 
 
-def total_steps(wires, terms, acc, above, below, beside, out):
+def total_steps(wires, terms, acc, above, below, beside, write):
     core = lax.rem(lax.axis_index("dp"), 2)
     z = lax.rem(lax.axis_index("dp") // 2, 8)
     xh = lax.axis_index("dp") // 16
@@ -224,7 +224,7 @@
     def last():
         state["far"].wait_recv()
         total = acc[xh * 8 + z].astype(F32) + above[3, xh].astype(F32)
-        out[...] = (total + below[3, xh].astype(F32) + beside[...].astype(F32)).astype(BF16)
+        write(total + below[3, xh].astype(F32) + beside[...].astype(F32))
 
     return start, first, middle(1), middle(2), middle(3), cross, last
 
@@ -326,8 +326,9 @@
 
 
 def kernel(
-    inputs, saved, attn, upstream, w_qkv, w_out, w_block,
-    grad_rows, qkv_sum, out_sum, conv_sum_a, conv_sum_b,
+    inputs, saved, attn, upstream, w_qkv, w_out, w_conv,
+    grad_rows, qkv_sum, grad_out, grad_conv,
+    w_block,
     saved_all, upstream_all, mid_pad, gelu_pad, attn_all, gelu_out_blocks, attn_blocks, slope,
     blocks, normed, proj, expo, sums, grad_attn, query_acc, grad_proj, parts, inbox,
     qkv_terms, out_terms, gelu_wide, w_taps, conv_a, conv_b, gelu_send, gelu_back,
@@ -372,6 +373,8 @@
     get_weight = weight_steps(wires, w_block, blocks)
     get_saved[0][0]()
     get_saved[1][0]()
+    taps_rows = [w_conv[tap].astype(F32) for tap in range(TAPS)]
+    w_block[...] = jnp.concatenate(taps_rows + [jnp.zeros((2, channels), F32)]).astype(BF16)
     get_weight[0]()
     kept = [
         pltpu.make_async_copy(saved, saved_all.at[span(here)], own_sems.at[0]),
@@ -534,8 +537,23 @@
     acts(seq_at(0, 0))
     both(5)
 
-    sum_qkv = total_steps(wires, qkv_terms, q0, q1, q2, q3, qkv_sum)
-    sum_out = total_steps(wires, out_terms, o0, o1, o2, o3, out_sum)
+    def write_qkv(total):
+        qkv_sum[...] = total.astype(BF16)
+
+    def write_out(total):
+        for part in range(2):
+            grad_out[:, pl.ds(part * half, half)] = total[6 * part : 6 * part + 6].astype(BF16)
+
+    def write_conv(part):
+        def write(total):
+            for tap in range(TAPS):
+                rows_of_tap = total[6 * tap : 6 * tap + 6].astype(BF16)
+                grad_conv[tap, :, pl.ds(part * half, half)] = rows_of_tap
+
+        return write
+
+    sum_qkv = total_steps(wires, qkv_terms, q0, q1, q2, q3, write_qkv)
+    sum_out = total_steps(wires, out_terms, o0, o1, o2, o3, write_out)
 
     def seq_qkv(first):
         @pl.loop(first, first + 2)
@@ -636,8 +654,8 @@
     get_mid[1][3]()
 
     totals = [
-        total_steps(wires, conv_a, a0, a1, a2, a3, conv_sum_a),
-        total_steps(wires, conv_b, b0, b1, b2, b3, conv_sum_b),
+        total_steps(wires, conv_a, a0, a1, a2, a3, write_conv(0)),
+        total_steps(wires, conv_b, b0, b1, b2, b3, write_conv(1)),
     ]
     for part, terms in enumerate((conv_a, conv_b)):
 
@@ -693,7 +711,7 @@
     wires.finish()
 
 
-def run(inputs, saved, attn, upstream, w_qkv, w_out, w_block):
+def run(inputs, saved, attn, upstream, w_qkv, w_out, w_conv):
     rows, channels = saved.shape
     length, width, half = 8 * rows, w_out.shape[0], channels // 2
     count = 2 * (3 * GATHER_SENDS + SCATTER_SENDS) + WEIGHT_SENDS + 3 * 7 + 4 * TOTAL_SENDS
@@ -703,13 +721,13 @@
         out_shape=[
             jax.ShapeDtypeStruct((rows, channels), BF16),
             jax.ShapeDtypeStruct((144, width), BF16),
-            jax.ShapeDtypeStruct((16, half), BF16),
-            jax.ShapeDtypeStruct((32, half), BF16),
-            jax.ShapeDtypeStruct((32, half), BF16),
+            jax.ShapeDtypeStruct((6, channels), BF16),
+            jax.ShapeDtypeStruct(w_conv.shape, BF16),
         ],
         in_specs=[in_vmem] * 7,
-        out_specs=[in_vmem] * 5,
+        out_specs=[in_vmem] * 4,
         scratch_shapes=[
+            VMEM((32, channels), BF16),
             VMEM((length, channels), BF16),
             VMEM((length, channels), BF16),
             VMEM((length + 2 * REACH, channels), BF16),
@@ -746,24 +764,15 @@
         compiler_params=pltpu.CompilerParams(
             collective_id=1, has_side_effects=True, vmem_limit_bytes=58 << 20
         ),
-    )(inputs, saved, attn, upstream, w_qkv, w_out, w_block)
+    )(inputs, saved, attn, upstream, w_qkv, w_out, w_conv)
 
 
 def local(inputs, saved, attn_saved, upstream, w_qkv, w_out, w_conv):
-    channels = inputs.shape[2]
-    width = w_out.shape[0]
-    taps_rows = w_conv.shape[0] * w_conv.shape[1]
-    w_block = jnp.pad(w_conv.reshape(taps_rows, channels), ((0, 32 - taps_rows), (0, 0)))
-    grad_rows, qkv_sum, out_sum, sum_a, sum_b = run(
-        inputs[0], saved[0], attn_saved[0], upstream[0], w_qkv.transpose(1, 2, 0), w_out, w_block
+    grad_rows, qkv_sum, grad_out, grad_conv = run(
+        inputs[0], saved[0], attn_saved[0], upstream[0], w_qkv.transpose(1, 2, 0), w_out, w_conv
     )
-    out_pair = out_sum[:12].reshape(2, 6, channels // 2)
-    return (
-        grad_rows[None],
-        qkv_sum.reshape(3, channels // 32, width).transpose(1, 0, 2),
-        jnp.concatenate([out_pair[0], out_pair[1]], axis=1),
-        jnp.concatenate([sum_a, sum_b], axis=1)[:taps_rows].reshape(w_conv.shape),
-    )
+    grad_qkv = qkv_sum.reshape(3, -1, w_out.shape[0]).transpose(1, 0, 2)
+    return grad_rows[None], grad_qkv, grad_out, grad_conv
 
 
 def solution(mesh):

time: 155 us -> 153 us (0.987)
    unnamed x2 -> x4, local copies, waits for them, and re-layouts: 3.29 us -> 6.19 us
    reshape x2 -> x0, local copies, waits for them, and re-layouts: 1.62 us -> none  [the longest x1 0.93 us: local(): w_conv.reshape(taps_rows, channels)]
where the time goes in v2:
time: 153 us
  Pallas kernels  146 us (95%)
  local copies, waits for them, and re-layouts  6.19 us (4%)
    pallas_call x1, Pallas kernels, run(): pl.pallas_call(kernel, out_shape=[jax.ShapeDtypeStruct((rows, channels),...  146 us
    unnamed x4, local copies, waits for them, and re-layouts  6.19 us

profile of v2, /device:TPU:8, one launch (start us, length us, event | category | flops | bytes accessed | tf_op | source)
XLA Modules:
  0.0 153.1 jit_solution(14787638158078734455)
XLA Ops:
  0.6 146.3 %shard_map.102 = (bf16[128,1536]{1,0:T(8,128)(2,1)}, bf16[144,192]{1,0:T(8,128)(2,1)}, bf16[6,1536]{1,0:T(8,128)(2,1)}, bf16[5,6,1536]{2,1,0:T(8,128)(2,1)}) custom-call(bf16[128,1536]{1,0:T(8,128)(2,1)} %bitcast.11, bf16[128,1536]{1,0:T(8,128)(2,1)} %bitcast.12, bf16[128,1536]{1,0:T(8,128)(2,1)} %bitcast.13, bf16[128,1536]{1,0:T(8,128)(2,1)} %bitcast.14, ...), custom_call_target="tpu_custom_call" | custom-call | tf_op jit(solution)/shard_map/pallas_call | solution.py:719
  147.0 1.8 %copy.15 = bf16[1,128,1536]{2,1,0:T(8,128)(2,1)} copy(bf16[1,128,1536]{2,1,0:T(8,128)(2,1)} %bitcast.10) | data formatting | bytes 786432
  148.7 1.5 copy.16
  150.2 1.3 copy.17
  151.6 1.6 %copy.18 = bf16[5,6,1536]{2,1,0:T(8,128)(2,1)} copy(bf16[5,6,1536]{2,1,0:T(8,128)(2,1)} %get-tuple-element.19) | data formatting | bytes 184320

commit v3 on v2

--- a/solution.py
+++ b/solution.py
@@ -767,10 +767,31 @@
     )(inputs, saved, attn, upstream, w_qkv, w_out, w_conv)
 
 
+def hand_over_kernel(a, b, c, d, a_out, b_out, c_out, d_out, done):
+    pairs = ((a, a_out), (b, b_out), (c, c_out), (d, d_out))
+    copies = [pltpu.make_async_copy(*pair, done.at[i]) for i, pair in enumerate(pairs)]
+    for copy in copies:
+        copy.start()
+    for copy in copies:
+        copy.wait()
+
+
+def hand_over(*results):
+    anywhere = pl.BlockSpec(memory_space=ANY)
+    return pl.pallas_call(
+        hand_over_kernel,
+        out_shape=[jax.ShapeDtypeStruct(result.shape, result.dtype) for result in results],
+        in_specs=[pl.BlockSpec(memory_space=VMEM)] * 4,
+        out_specs=[anywhere] * 4,
+        scratch_shapes=[pltpu.SemaphoreType.DMA((4,))],
+    )(*results)
+
+
 def local(inputs, saved, attn_saved, upstream, w_qkv, w_out, w_conv):
-    grad_rows, qkv_sum, grad_out, grad_conv = run(
+    results = run(
         inputs[0], saved[0], attn_saved[0], upstream[0], w_qkv.transpose(1, 2, 0), w_out, w_conv
     )
+    grad_rows, qkv_sum, grad_out, grad_conv = hand_over(*results)
     grad_qkv = qkv_sum.reshape(3, -1, w_out.shape[0]).transpose(1, 0, 2)
     return grad_rows[None], grad_qkv, grad_out, grad_conv
 

time: 153 us -> 149 us (0.974)
  local copies, waits for them, and re-layouts: 6.19 us -> 0 us
  Pallas kernels: 146 us -> 148 us
    unnamed x4 -> x0, local copies, waits for them, and re-layouts: 6.19 us -> none
    pallas_call x0 -> x1, Pallas kernels: none -> 1.92 us  [hand_over(): pl.pallas_call(hand_over_kernel, out_shape=[jax.ShapeDtypeStruct(result.s...]
where the time goes in v3:
time: 149 us
  Pallas kernels  148 us (99%)
    pallas_call x1, Pallas kernels, run(): pl.pallas_call(kernel, out_shape=[jax.ShapeDtypeStruct((rows, channels),...  146 us

profile of v3, /device:TPU:8, one launch (start us, length us, event | category | flops | bytes accessed | tf_op | source)
XLA Modules:
  0.0 149.0 jit_solution(16267648596340449535)
XLA Ops:
  0.6 146.3 %shard_map.102 = (bf16[128,1536]{1,0:T(8,128)(2,1)}, bf16[144,192]{1,0:T(8,128)(2,1)}, bf16[6,1536]{1,0:T(8,128)(2,1)}, bf16[5,6,1536]{2,1,0:T(8,128)(2,1)}) custom-call(bf16[128,1536]{1,0:T(8,128)(2,1)} %bitcast.10, bf16[128,1536]{1,0:T(8,128)(2,1)} %bitcast.11, bf16[128,1536]{1,0:T(8,128)(2,1)} %bitcast.12, bf16[128,1536]{1,0:T(8,128)(2,1)} %bitcast.13, ...), custom_call_target="tpu_custom_call" | custom-call | tf_op jit(solution)/shard_map/pallas_call | solution.py:719
  146.9 1.9 %shard_map.103 = (bf16[128,1536]{1,0:T(8,128)(2,1)}, bf16[144,192]{1,0:T(8,128)(2,1)}, bf16[6,1536]{1,0:T(8,128)(2,1)}, bf16[5,6,1536]{2,1,0:T(8,128)(2,1)}) custom-call(bf16[128,1536]{1,0:T(8,128)(2,1)} %get-tuple-element.12.a, bf16[144,192]{1,0:T(8,128)(2,1)} %get-tuple-element.13.b, bf16[6,1536]{1,0:T(8,128)(2,1)} %get-tuple-element.14.c, ...), custom_call_target="tpu_custom_call" | custom-call | tf_op jit(solution)/shard_map/pallas_call | solution.py:781
